TPU v7x, 256 devices: a whole 4x4x8 slice. The times are simulated.
256 devices in a mesh: blk: 32 (over z, x_lo, core), head: 8 (over x_hi, y).
Axes of the slice: x: 4 (x_hi: 2, x_lo: 2; x = x_hi * 2 + x_lo), y: 4, z: 8, core: 2. Of those that a mesh axis runs over, the one named last changes fastest.
Arguments:
- queries: bfloat16 [131072, 512], P(('blk', 'head')), may hold values from -6 to 6
- keys: bfloat16 [131072, 512], P(('blk', 'head')), may hold values from -6 to 6
- values: bfloat16 [131072, 512], P(('blk', 'head')), may hold values from -6 to 6
- w_out: bfloat16 [512, 512], replicated, may hold values from -3 to 3
Outputs:
- projected: bfloat16 [131072, 512], P(('blk', 'head'))
All inputs are finite; a program needn't handle non-finite values.
Results may differ from a plain program's by a relative error of at most 0.0054.
Values may be sent and summed in bfloat16 or wider, within the bound.
A program may use at most 128 MiB of HBM per device.

v0:
```python
import jax
import jax.numpy as jnp
from jax import lax
from jax.sharding import PartitionSpec as P

HEADS = 8
HEAD_DIM = 64


scaling = 0.125


def from_behind(array, axis, by):
    size = lax.axis_size(axis)
    return lax.ppermute(array, axis, [(i, (i + by) % size) for i in range(size)])


def attend(queries, keys, values):
    rows, heads, size = queries.shape
    step = 512
    q_heads = jnp.transpose(queries, (1, 0, 2)).reshape(heads, rows // step, step, size)
    k_heads = jnp.transpose(keys, (1, 0, 2))
    v_heads = jnp.transpose(values, (1, 0, 2))

    def per_head(items):
        q_one, k_one, v_one = items

        def per_block(q_block):
            scores = jnp.dot(q_block, k_one.T, preferred_element_type=jnp.float32) * scaling
            top = jnp.max(scores, axis=1, keepdims=True)
            expo = jnp.exp(scores - top)
            total = jnp.sum(expo, axis=1, keepdims=True)
            probs = expo.astype(jnp.bfloat16)
            mixed = jnp.dot(probs, v_one, preferred_element_type=jnp.float32) / total
            return mixed.astype(jnp.bfloat16)

        return lax.map(per_block, q_one)

    result = lax.map(per_head, (q_heads, k_heads, v_heads))
    return jnp.transpose(result.reshape(heads, rows, size), (1, 0, 2))


def on_device(queries, keys, values, w_out):
    rows = queries.shape[0]
    group_k, group_v = (
        lax.all_gather(keys, "head", axis=0, tiled=True),
        lax.all_gather(values, "head", axis=0, tiled=True),
    )
    next_k, next_v = from_behind((group_k, group_v), "blk", -1)
    window_k = jnp.concatenate([group_k, next_k], axis=0).reshape(-1, HEADS, HEAD_DIM)
    window_v = jnp.concatenate([group_v, next_v], axis=0).reshape(-1, HEADS, HEAD_DIM)
    mixed = attend(queries.reshape(rows, HEADS, HEAD_DIM), window_k, window_v).reshape(
        rows, HEADS * HEAD_DIM
    )
    return jnp.dot(mixed, w_out, preferred_element_type=jnp.float32).astype(jnp.bfloat16)


def solution(mesh):
    in_specs = (P(("blk", "head"), None), P(("blk", "head"), None), P(("blk", "head"), None), P())
    out_specs = P(("blk", "head"), None)
    return jax.shard_map(
        on_device, mesh=mesh, in_specs=in_specs, out_specs=out_specs, check_vma=False
    )
```

profile of v0, /device:TPU:224, one launch (start us, length us, event | category | flops | bytes accessed | tf_op | source)
XLA Modules:
  0.0 478.1 jit_solution(1123322217130528171)
XLA Ops:
  6.5 0.0 copy-start
  6.5 0.0 all-gather.5.cloned.1.call-start
  6.5 2.1 copy.7
  8.7 0.0 all-gather.5.cloned.1.call-update
  8.7 0.0 all-gather.3.cloned.1.call-start
  8.8 2.0 copy.6
  10.8 0.0 all-gather.3.cloned.1.call-update
  10.8 78.2 %all-gather.5.cloned.1.call-done = bf16[4096,512]{0,1:T(8,128)(2,1)} async-done(((bf16[512,512]{0,1:T(8,128)(2,1)}), bf16[4096,512]{0,1:T(8,128)(2,1)}) %all-gather.5.cloned.1.call-update) | async-done | bytes 4194320 | tf_op jit(solution)/shard_map/all_gather | solution.py:47
  89.0 0.4 collective-permute-start.1
  89.4 110.3 %all-gather.3.cloned.1.call-done = bf16[4096,512]{0,1:T(8,128)(2,1)} async-done(((bf16[512,512]{0,1:T(8,128)(2,1)}), bf16[4096,512]{0,1:T(8,128)(2,1)}) %all-gather.3.cloned.1.call-update) | async-done | bytes 4194320 | tf_op jit(solution)/shard_map/all_gather | solution.py:46
  199.7 0.4 collective-permute-start
  200.1 1.3 copy.5
  201.4 0.0 collective-permute-done.1
  201.4 7.7 %pad_maximum_fusion.1 = bf16[8192,512]{0,1:T(8,128)(2,1)} fusion(bf16[4096,512]{0,1:T(8,128)(2,1)} %collective-permute-done.1, bf16[4096,512]{0,1:T(8,128)(2,1)} %all-gather.5.cloned.1.call-done), kind=kLoop, calls=%fused_computation.20 | loop fusion | flops 16777216 | bytes 16777216 | tf_op jit(solution)/shard_map/concatenate | solution.py:51
  209.1 37.4 %collective-permute-done = bf16[4096,512]{0,1:T(8,128)(2,1)} collective-permute-done((bf16[4096,512]{0,1:T(8,128)(2,1)}, bf16[4096,512]{0,1:T(8,128)(2,1)}, u32[]{:S(2)}, u32[]{:S(2)}) %collective-permute-start) | collective-permute-done | bytes 4194336 | tf_op jit(solution)/shard_map/ppermute | solution.py:15
  246.5 7.7 %pad_maximum_fusion = bf16[8192,512]{0,1:T(8,128)(2,1)} fusion(bf16[4096,512]{0,1:T(8,128)(2,1)} %collective-permute-done, bf16[4096,512]{0,1:T(8,128)(2,1)} %all-gather.3.cloned.1.call-done), kind=kLoop, calls=%fused_computation.19 | loop fusion | flops 16777216 | bytes 16777216 | tf_op jit(solution)/shard_map/concatenate | solution.py:50
  254.2 215.8 %while.10 = (s32[]{:T(128)}, bf16[8,1,512,64]{2,3,1,0:T(8,128)(2,1)S(1)}, bf16[8,1,512,64]{2,3,0,1:T(8,128)(2,1)S(1)}, bf16[8,8192,64]{1,2,0:T(8,128)(2,1)}, bf16[8,8192,64]{1,2,0:T(8,128)(2,1)}, /*index=5*/s32[]{:T(128)}) while((s32[]{:T(128)}, bf16[8,1,512,64]{2,3,1,0:T(8,128)(2,1)S(1)}, bf16[8,1,512,64]{2,3,0,1:T(8,128)(2,1)S(1)}, ...), condition=%wide.region_3.4_spmd, body=%wide.region_0.3_spmd.sunk | while | flops 1107360768 | bytes 52572228 | solution.py:39
  254.2 9.3 %multiply_reduce_fusion.2 = (f32[512]{0:T(512)S(1)}, f32[512,8192]{1,0:T(8,128)}) fusion(bf16[8,8192,64]{1,2,0:T(8,128)(2,1)} %get-tuple-element.115, s32[]{:T(128)} %get-tuple-element.106, bf16[8,1,512,64]{2,3,0,1:T(8,128)(2,1)S(1)} %get-tuple-element.114), kind=kOutput, calls=%fused_computation.1.clone.1 | convolution fusion | flops 545259008 | bytes 17894400 | tf_op jit(solution)/shard_map/while/body/eval_jaxpr/while/body/eval_jaxpr/dot_general | solution.py:29
  263.5 8.6 %fusion.34 = f32[512]{0:T(512)S(1)} fusion(f32[512,8192]{1,0:T(8,128)} %get-tuple-element.98, f32[512]{0:T(512)S(1)} %get-tuple-element.99), kind=kLoop, calls=%fused_computation.2.clone.1 | loop fusion | flops 12582400 | bytes 16781312 | tf_op jit(solution)/shard_map/while/body/eval_jaxpr/while/body/eval_jaxpr/reduce_sum | solution.py:32
  272.1 9.0 %fusion.35 = bf16[8,1,512,64]{2,3,1,0:T(8,128)(2,1)S(1)} fusion(bf16[8,1,512,64]{2,3,1,0:T(8,128)(2,1)S(1)} %get-tuple-element.107, s32[]{:T(128)} %get-tuple-element.106, f32[512,8192]{1,0:T(8,128)} %get-tuple-element.98, f32[512]{0:T(512)S(1)} %get-tuple-element.99, bf16[8,8192,64]{1,2,0:T(8,128)(2,1)} %get-tuple-element.116, f32[512]{0:T(512)S(1)} %fusion.34), kind=kOutput, calls=%fused_computation.8.clone.1 | convolution fusion | flops 549519360 | bytes 17896448 | tf_op jit(solution)/shard_map/while/body/eval_jaxpr/while/body/eval_jaxpr/dot_general | solution.py:34
  281.1 9.3 %multiply_reduce_fusion.2 = (f32[512]{0:T(512)S(1)}, f32[512,8192]{1,0:T(8,128)}) fusion(bf16[8,8192,64]{1,2,0:T(8,128)(2,1)} %get-tuple-element.115, s32[]{:T(128)} %get-tuple-element.106, bf16[8,1,512,64]{2,3,0,1:T(8,128)(2,1)S(1)} %get-tuple-element.114), kind=kOutput, calls=%fused_computation.1.clone.1 | convolution fusion | flops 545259008 | bytes 17894400 | tf_op jit(solution)/shard_map/while/body/eval_jaxpr/while/body/eval_jaxpr/dot_general | solution.py:29
  290.5 8.6 %fusion.34 = f32[512]{0:T(512)S(1)} fusion(f32[512,8192]{1,0:T(8,128)} %get-tuple-element.98, f32[512]{0:T(512)S(1)} %get-tuple-element.99), kind=kLoop, calls=%fused_computation.2.clone.1 | loop fusion | flops 12582400 | bytes 16781312 | tf_op jit(solution)/shard_map/while/body/eval_jaxpr/while/body/eval_jaxpr/reduce_sum | solution.py:32
  299.1 9.0 %fusion.35 = bf16[8,1,512,64]{2,3,1,0:T(8,128)(2,1)S(1)} fusion(bf16[8,1,512,64]{2,3,1,0:T(8,128)(2,1)S(1)} %get-tuple-element.107, s32[]{:T(128)} %get-tuple-element.106, f32[512,8192]{1,0:T(8,128)} %get-tuple-element.98, f32[512]{0:T(512)S(1)} %get-tuple-element.99, bf16[8,8192,64]{1,2,0:T(8,128)(2,1)} %get-tuple-element.116, f32[512]{0:T(512)S(1)} %fusion.34), kind=kOutput, calls=%fused_computation.8.clone.1 | convolution fusion | flops 549519360 | bytes 17896448 | tf_op jit(solution)/shard_map/while/body/eval_jaxpr/while/body/eval_jaxpr/dot_general | solution.py:34
  308.1 9.3 %multiply_reduce_fusion.2 = (f32[512]{0:T(512)S(1)}, f32[512,8192]{1,0:T(8,128)}) fusion(bf16[8,8192,64]{1,2,0:T(8,128)(2,1)} %get-tuple-element.115, s32[]{:T(128)} %get-tuple-element.106, bf16[8,1,512,64]{2,3,0,1:T(8,128)(2,1)S(1)} %get-tuple-element.114), kind=kOutput, calls=%fused_computation.1.clone.1 | convolution fusion | flops 545259008 | bytes 17894400 | tf_op jit(solution)/shard_map/while/body/eval_jaxpr/while/body/eval_jaxpr/dot_general | solution.py:29
  317.4 8.6 %fusion.34 = f32[512]{0:T(512)S(1)} fusion(f32[512,8192]{1,0:T(8,128)} %get-tuple-element.98, f32[512]{0:T(512)S(1)} %get-tuple-element.99), kind=kLoop, calls=%fused_computation.2.clone.1 | loop fusion | flops 12582400 | bytes 16781312 | tf_op jit(solution)/shard_map/while/body/eval_jaxpr/while/body/eval_jaxpr/reduce_sum | solution.py:32
  326.0 9.0 %fusion.35 = bf16[8,1,512,64]{2,3,1,0:T(8,128)(2,1)S(1)} fusion(bf16[8,1,512,64]{2,3,1,0:T(8,128)(2,1)S(1)} %get-tuple-element.107, s32[]{:T(128)} %get-tuple-element.106, f32[512,8192]{1,0:T(8,128)} %get-tuple-element.98, f32[512]{0:T(512)S(1)} %get-tuple-element.99, bf16[8,8192,64]{1,2,0:T(8,128)(2,1)} %get-tuple-element.116, f32[512]{0:T(512)S(1)} %fusion.34), kind=kOutput, calls=%fused_computation.8.clone.1 | convolution fusion | flops 549519360 | bytes 17896448 | tf_op jit(solution)/shard_map/while/body/eval_jaxpr/while/body/eval_jaxpr/dot_general | solution.py:34
  335.1 9.3 %multiply_reduce_fusion.2 = (f32[512]{0:T(512)S(1)}, f32[512,8192]{1,0:T(8,128)}) fusion(bf16[8,8192,64]{1,2,0:T(8,128)(2,1)} %get-tuple-element.115, s32[]{:T(128)} %get-tuple-element.106, bf16[8,1,512,64]{2,3,0,1:T(8,128)(2,1)S(1)} %get-tuple-element.114), kind=kOutput, calls=%fused_computation.1.clone.1 | convolution fusion | flops 545259008 | bytes 17894400 | tf_op jit(solution)/shard_map/while/body/eval_jaxpr/while/body/eval_jaxpr/dot_general | solution.py:29
  344.4 8.6 %fusion.34 = f32[512]{0:T(512)S(1)} fusion(f32[512,8192]{1,0:T(8,128)} %get-tuple-element.98, f32[512]{0:T(512)S(1)} %get-tuple-element.99), kind=kLoop, calls=%fused_computation.2.clone.1 | loop fusion | flops 12582400 | bytes 16781312 | tf_op jit(solution)/shard_map/while/body/eval_jaxpr/while/body/eval_jaxpr/reduce_sum | solution.py:32
  353.0 9.0 %fusion.35 = bf16[8,1,512,64]{2,3,1,0:T(8,128)(2,1)S(1)} fusion(bf16[8,1,512,64]{2,3,1,0:T(8,128)(2,1)S(1)} %get-tuple-element.107, s32[]{:T(128)} %get-tuple-element.106, f32[512,8192]{1,0:T(8,128)} %get-tuple-element.98, f32[512]{0:T(512)S(1)} %get-tuple-element.99, bf16[8,8192,64]{1,2,0:T(8,128)(2,1)} %get-tuple-element.116, f32[512]{0:T(512)S(1)} %fusion.34), kind=kOutput, calls=%fused_computation.8.clone.1 | convolution fusion | flops 549519360 | bytes 17896448 | tf_op jit(solution)/shard_map/while/body/eval_jaxpr/while/body/eval_jaxpr/dot_general | solution.py:34
  362.1 9.3 %multiply_reduce_fusion.2 = (f32[512]{0:T(512)S(1)}, f32[512,8192]{1,0:T(8,128)}) fusion(bf16[8,8192,64]{1,2,0:T(8,128)(2,1)} %get-tuple-element.115, s32[]{:T(128)} %get-tuple-element.106, bf16[8,1,512,64]{2,3,0,1:T(8,128)(2,1)S(1)} %get-tuple-element.114), kind=kOutput, calls=%fused_computation.1.clone.1 | convolution fusion | flops 545259008 | bytes 17894400 | tf_op jit(solution)/shard_map/while/body/eval_jaxpr/while/body/eval_jaxpr/dot_general | solution.py:29
  371.4 8.6 %fusion.34 = f32[512]{0:T(512)S(1)} fusion(f32[512,8192]{1,0:T(8,128)} %get-tuple-element.98, f32[512]{0:T(512)S(1)} %get-tuple-element.99), kind=kLoop, calls=%fused_computation.2.clone.1 | loop fusion | flops 12582400 | bytes 16781312 | tf_op jit(solution)/shard_map/while/body/eval_jaxpr/while/body/eval_jaxpr/reduce_sum | solution.py:32
  380.0 9.0 %fusion.35 = bf16[8,1,512,64]{2,3,1,0:T(8,128)(2,1)S(1)} fusion(bf16[8,1,512,64]{2,3,1,0:T(8,128)(2,1)S(1)} %get-tuple-element.107, s32[]{:T(128)} %get-tuple-element.106, f32[512,8192]{1,0:T(8,128)} %get-tuple-element.98, f32[512]{0:T(512)S(1)} %get-tuple-element.99, bf16[8,8192,64]{1,2,0:T(8,128)(2,1)} %get-tuple-element.116, f32[512]{0:T(512)S(1)} %fusion.34), kind=kOutput, calls=%fused_computation.8.clone.1 | convolution fusion | flops 549519360 | bytes 17896448 | tf_op jit(solution)/shard_map/while/body/eval_jaxpr/while/body/eval_jaxpr/dot_general | solution.py:34
  389.0 9.3 %multiply_reduce_fusion.2 = (f32[512]{0:T(512)S(1)}, f32[512,8192]{1,0:T(8,128)}) fusion(bf16[8,8192,64]{1,2,0:T(8,128)(2,1)} %get-tuple-element.115, s32[]{:T(128)} %get-tuple-element.106, bf16[8,1,512,64]{2,3,0,1:T(8,128)(2,1)S(1)} %get-tuple-element.114), kind=kOutput, calls=%fused_computation.1.clone.1 | convolution fusion | flops 545259008 | bytes 17894400 | tf_op jit(solution)/shard_map/while/body/eval_jaxpr/while/body/eval_jaxpr/dot_general | solution.py:29
  398.4 8.6 %fusion.34 = f32[512]{0:T(512)S(1)} fusion(f32[512,8192]{1,0:T(8,128)} %get-tuple-element.98, f32[512]{0:T(512)S(1)} %get-tuple-element.99), kind=kLoop, calls=%fused_computation.2.clone.1 | loop fusion | flops 12582400 | bytes 16781312 | tf_op jit(solution)/shard_map/while/body/eval_jaxpr/while/body/eval_jaxpr/reduce_sum | solution.py:32
  407.0 9.0 %fusion.35 = bf16[8,1,512,64]{2,3,1,0:T(8,128)(2,1)S(1)} fusion(bf16[8,1,512,64]{2,3,1,0:T(8,128)(2,1)S(1)} %get-tuple-element.107, s32[]{:T(128)} %get-tuple-element.106, f32[512,8192]{1,0:T(8,128)} %get-tuple-element.98, f32[512]{0:T(512)S(1)} %get-tuple-element.99, bf16[8,8192,64]{1,2,0:T(8,128)(2,1)} %get-tuple-element.116, f32[512]{0:T(512)S(1)} %fusion.34), kind=kOutput, calls=%fused_computation.8.clone.1 | convolution fusion | flops 549519360 | bytes 17896448 | tf_op jit(solution)/shard_map/while/body/eval_jaxpr/while/body/eval_jaxpr/dot_general | solution.py:34
  416.0 9.3 %multiply_reduce_fusion.2 = (f32[512]{0:T(512)S(1)}, f32[512,8192]{1,0:T(8,128)}) fusion(bf16[8,8192,64]{1,2,0:T(8,128)(2,1)} %get-tuple-element.115, s32[]{:T(128)} %get-tuple-element.106, bf16[8,1,512,64]{2,3,0,1:T(8,128)(2,1)S(1)} %get-tuple-element.114), kind=kOutput, calls=%fused_computation.1.clone.1 | convolution fusion | flops 545259008 | bytes 17894400 | tf_op jit(solution)/shard_map/while/body/eval_jaxpr/while/body/eval_jaxpr/dot_general | solution.py:29
  425.3 8.6 %fusion.34 = f32[512]{0:T(512)S(1)} fusion(f32[512,8192]{1,0:T(8,128)} %get-tuple-element.98, f32[512]{0:T(512)S(1)} %get-tuple-element.99), kind=kLoop, calls=%fused_computation.2.clone.1 | loop fusion | flops 12582400 | bytes 16781312 | tf_op jit(solution)/shard_map/while/body/eval_jaxpr/while/body/eval_jaxpr/reduce_sum | solution.py:32
  434.0 9.0 %fusion.35 = bf16[8,1,512,64]{2,3,1,0:T(8,128)(2,1)S(1)} fusion(bf16[8,1,512,64]{2,3,1,0:T(8,128)(2,1)S(1)} %get-tuple-element.107, s32[]{:T(128)} %get-tuple-element.106, f32[512,8192]{1,0:T(8,128)} %get-tuple-element.98, f32[512]{0:T(512)S(1)} %get-tuple-element.99, bf16[8,8192,64]{1,2,0:T(8,128)(2,1)} %get-tuple-element.116, f32[512]{0:T(512)S(1)} %fusion.34), kind=kOutput, calls=%fused_computation.8.clone.1 | convolution fusion | flops 549519360 | bytes 17896448 | tf_op jit(solution)/shard_map/while/body/eval_jaxpr/while/body/eval_jaxpr/dot_general | solution.py:34
  443.0 9.3 %multiply_reduce_fusion.2 = (f32[512]{0:T(512)S(1)}, f32[512,8192]{1,0:T(8,128)}) fusion(bf16[8,8192,64]{1,2,0:T(8,128)(2,1)} %get-tuple-element.115, s32[]{:T(128)} %get-tuple-element.106, bf16[8,1,512,64]{2,3,0,1:T(8,128)(2,1)S(1)} %get-tuple-element.114), kind=kOutput, calls=%fused_computation.1.clone.1 | convolution fusion | flops 545259008 | bytes 17894400 | tf_op jit(solution)/shard_map/while/body/eval_jaxpr/while/body/eval_jaxpr/dot_general | solution.py:29
  452.3 8.6 %fusion.34 = f32[512]{0:T(512)S(1)} fusion(f32[512,8192]{1,0:T(8,128)} %get-tuple-element.98, f32[512]{0:T(512)S(1)} %get-tuple-element.99), kind=kLoop, calls=%fused_computation.2.clone.1 | loop fusion | flops 12582400 | bytes 16781312 | tf_op jit(solution)/shard_map/while/body/eval_jaxpr/while/body/eval_jaxpr/reduce_sum | solution.py:32
  460.9 9.0 %fusion.35 = bf16[8,1,512,64]{2,3,1,0:T(8,128)(2,1)S(1)} fusion(bf16[8,1,512,64]{2,3,1,0:T(8,128)(2,1)S(1)} %get-tuple-element.107, s32[]{:T(128)} %get-tuple-element.106, f32[512,8192]{1,0:T(8,128)} %get-tuple-element.98, f32[512]{0:T(512)S(1)} %get-tuple-element.99, bf16[8,8192,64]{1,2,0:T(8,128)(2,1)} %get-tuple-element.116, f32[512]{0:T(512)S(1)} %fusion.34), kind=kOutput, calls=%fused_computation.8.clone.1 | convolution fusion | flops 549519360 | bytes 17896448 | tf_op jit(solution)/shard_map/while/body/eval_jaxpr/while/body/eval_jaxpr/dot_general | solution.py:34
  470.0 0.0 copy-done
  470.0 1.3 convolution_convert_fusion
  (1 shorter events, 0.0 us)
Async XLA Ops:
  6.5 463.4 %copy-start = (bf16[512,512]{1,0:T(8,128)(2,1)S(1)}, bf16[512,512]{1,0:T(8,128)(2,1)}, u32[]{:S(2)}) copy-start(bf16[512,512]{1,0:T(8,128)(2,1)} %param.9) | copy-start | bytes 1572868
  6.5 82.5 %all-gather.5.cloned.1.call-start = ((), (), s32[]{:S(2)}) async-start(), calls=%async_computation.1 | async-start | bytes 4718592 | tf_op jit(solution)/shard_map/all_gather | solution.py:47
  8.7 191.0 %all-gather.3.cloned.1.call-start = ((), (), s32[]{:S(2)}) async-start(), calls=%async_computation | async-start | bytes 4718592 | tf_op jit(solution)/shard_map/all_gather | solution.py:46
  89.0 112.4 %collective-permute-start.1 = (bf16[4096,512]{0,1:T(8,128)(2,1)}, bf16[4096,512]{0,1:T(8,128)(2,1)}, u32[]{:S(2)}, u32[]{:S(2)}) collective-permute-start(bf16[4096,512]{0,1:T(8,128)(2,1)} %all-gather.5.cloned.1.call-done), channel_id=1, source_target_pairs={{0,248},{8,0},{16,8},{24,16},{32,24},{40,32},{48,40},{56,48},{64,5... | collective-permute-start | bytes 12582920 | tf_op jit(solution)/shard_map/ppermute | solution.py:15
  199.7 46.8 %collective-permute-start = (bf16[4096,512]{0,1:T(8,128)(2,1)}, bf16[4096,512]{0,1:T(8,128)(2,1)}, u32[]{:S(2)}, u32[]{:S(2)}) collective-permute-start(bf16[4096,512]{0,1:T(8,128)(2,1)} %all-gather.3.cloned.1.call-done), channel_id=1, source_target_pairs={{0,248},{8,0},{16,8},{24,16},{32,24},{40,32},{48,40},{56,48},{64,5... | collective-permute-start | bytes 12582920 | tf_op jit(solution)/shard_map/ppermute | solution.py:15
Sparse Core Ops, SparseCore 0:
  9.8 79.1 all-gather.4
  91.5 108.2 all-gather.2
where the time goes:
time: 483 us; the launch traced here: 478 us
  waiting for transfers between devices  226 us (47%)
  matrix products  148 us (31%)
  other arithmetic  84.3 us (17%)
  between operations  13.4 us (3%)
  local copies, waits for them, and re-layouts  5.45 us (1%)
    all_gather x1, waiting for transfers between devices, on_device(): lax.all_gather(keys, 'head', axis=0, tiled=True)  110 us
    all_gather x1, waiting for transfers between devices, on_device(): lax.all_gather(values, 'head', axis=0, tiled=True)  78.2 us
    dot_general x8, matrix products, per_block(): jnp.dot(q_block, k_one.T, preferred_element_type=jnp.float32) * scaling  74.5 us
    dot_general x8, matrix products, per_block(): mixed = jnp.dot(probs, v_one, preferred_element_type=jnp.float32) / total  72.2 us
    reduce_sum x8, other arithmetic, per_block(): total = jnp.sum(expo, axis=1, keepdims=True)  68.9 us
    ppermute x2, waiting for transfers between devices, from_behind(): lax.ppermute(array, axis, [(i, (i + by) % size) for i in range(size)])  37.4 us
  transfers between devices with their start and end apart: 4, of which 3 were waited for; matrix products, arithmetic and copies ran while one was open for 2% of the time, Pallas kernels for 0%

commit v1 on v0

v1 whole, which is shorter than its diff:
```python
import jax
import jax.numpy as jnp
from jax import lax
from jax.experimental import pallas as pl
from jax.experimental.pallas import tpu as pltpu
from jax.sharding import PartitionSpec as P

HEADS = 8
HEAD_DIM = 64
TOK = 512
N_BLK = 32
WIDE = HEADS * HEAD_DIM
VROWS = 80
SUB = 256
GROUP = 4
TILE = GROUP * TOK
SCALE = 0.125 * 1.4426950408889634
F32 = jnp.float32
BF16 = jnp.bfloat16
MESH = pl.DeviceIdType.MESH
Y_FIRST = (1, 3, 2, 4, 5, 7, 6)


def mirror(r):
    if isinstance(r, int):
        return (r // 4) * 4 + (4 - r % 4) % 4
    return lax.div(r, 4) * 4 + lax.rem(4 - lax.rem(r, 4), 4)


def kernel(
    q_ref, k_ref, v_ref, w_ref, out_ref,
    q_send, k_send, v_send, q_in, k_in, v_in, q_wide, k_wide,
    acc, top, s_even, s_odd, o_send, o_in,
    q_ss, q_rs, k_ss, k_rs, v_ss, v_rs, o_ss, o_rs,
):
    blk = lax.axis_index("blk")
    head = lax.axis_index("head")
    before = lax.rem(blk + N_BLK - 1, N_BLK)
    behind = lax.rem(blk + 1, N_BLK)

    def peer(r):
        far = lax.rem(head // 4 + r // 4, 2)
        near = lax.rem(lax.rem(head, 4) + lax.rem(r, 4), 4)
        return far * 4 + near

    barrier = pltpu.get_barrier_semaphore()
    for r in Y_FIRST:
        pl.semaphore_signal(barrier, inc=1, device_id=(blk, peer(r)), device_id_type=MESH)
    pl.semaphore_signal(barrier, inc=1, device_id=(behind, head), device_id_type=MESH)

    def send_q(r):
        p, s = peer(r), mirror(r)
        return pltpu.make_async_remote_copy(
            src_ref=q_send.at[p], dst_ref=q_in.at[s], send_sem=q_ss.at[r], recv_sem=q_rs.at[s],
            device_id=(blk, p), device_id_type=MESH)

    def send_k(r):
        p, s = peer(r), mirror(r)
        return pltpu.make_async_remote_copy(
            src_ref=k_send.at[p], dst_ref=k_in.at[s], send_sem=k_ss.at[r], recv_sem=k_rs.at[s],
            device_id=(blk, p), device_id_type=MESH)

    def send_v(r):
        p, s = peer(r), mirror(r)
        return pltpu.make_async_remote_copy(
            src_ref=v_send.at[p], dst_ref=v_in.at[s, pl.ds(0, HEAD_DIM)],
            send_sem=v_ss.at[r], recv_sem=v_rs.at[s],
            device_id=(blk, p), device_id_type=MESH)

    def pass_k(r):
        return pltpu.make_async_remote_copy(
            src_ref=k_in.at[r], dst_ref=k_in.at[8 + r], send_sem=k_ss.at[8 + r],
            recv_sem=k_rs.at[8 + r], device_id=(before, head), device_id_type=MESH)

    def pass_v(r):
        return pltpu.make_async_remote_copy(
            src_ref=v_in.at[r, pl.ds(0, HEAD_DIM)], dst_ref=v_in.at[8 + r, pl.ds(0, HEAD_DIM)],
            send_sem=v_ss.at[8 + r], recv_sem=v_rs.at[8 + r],
            device_id=(before, head), device_id_type=MESH)

    def send_o(r):
        return pltpu.make_async_remote_copy(
            src_ref=o_send.at[r], dst_ref=o_in.at[head], send_sem=o_ss.at[r], recv_sem=o_rs.at[head],
            device_id=(blk, peer(r)), device_id_type=MESH)

    half = TOK // 2
    left = lax.broadcasted_iota(jnp.int32, (half, 128), 1) < HEAD_DIM

    def swap(x):
        return pltpu.roll(x, HEAD_DIM, 1)

    for pair in range(HEADS // 2):
        cols = slice(pair * 128, pair * 128 + 128)
        a = k_ref[0:half, cols].astype(F32)
        b = k_ref[half:TOK, cols].astype(F32)
        k_send[2 * pair] = jnp.where(left, a, swap(b)).astype(BF16)
        k_send[2 * pair + 1] = jnp.where(left, swap(a), b).astype(BF16)
    pl.semaphore_wait(barrier, 8)
    for r in (1, 3, 2):
        send_k(r).start()

    def transpose_into(src, dst):
        for pair in range(HEADS // 2):
            t = src[:, pair * 128:pair * 128 + 128].T
            dst[2 * pair] = t[:HEAD_DIM]
            dst[2 * pair + 1] = t[HEAD_DIM:]

    transpose_into(v_ref, v_send)
    for r in (1, 3, 2):
        send_v(r).start()
    transpose_into(q_ref, q_send)
    for r in Y_FIRST:
        send_q(r).start()
    for r in (4, 5, 7, 6):
        send_k(r).start()
        send_v(r).start()

    k_in[0] = k_send[head]
    v_in[0, 0:HEAD_DIM] = v_send[head]
    pass_k(0).start()
    pass_v(0).start()
    for s in range(16):
        v_in[s, HEAD_DIM:VROWS] = jnp.ones((VROWS - HEAD_DIM, TOK), BF16)

    def widen_q(q, s):
        scaled = q.astype(F32) * SCALE
        high = scaled.astype(BF16)
        q_wide[s, 0:HEAD_DIM] = high
        q_wide[s, HEAD_DIM:2 * HEAD_DIM] = (scaled - high.astype(F32)).astype(BF16)

    def widen_k(s):
        x = k_in[s].astype(F32)
        y = swap(x)
        k_wide[s, 0:half] = jnp.where(left, x, y).astype(BF16)
        k_wide[s, half:TOK] = jnp.where(left, y, x).astype(BF16)

    widen_q(q_send[head], 0)
    widen_k(0)
    acc[...] = jnp.zeros_like(acc)
    top[...] = jnp.full(top.shape, -1e30, F32)

    def arrive(r):
        send_k(mirror(r)).wait_recv()
        send_v(mirror(r)).wait_recv()
        pass_k(r).start()
        pass_v(r).start()
        widen_k(r)

    def arrive_next(r):
        pass_k(r).wait_recv()
        pass_v(r).wait_recv()
        widen_k(8 + r)

    for r in (1, 3, 2):
        arrive(r)

    def where(t):
        g = t // 8
        return lax.rem(t + g // 3, 8), g

    def scores(dst, t):
        i, g = where(t)
        q = q_wide[i]
        most = None
        for u in range(TILE // SUB):
            k = k_wide[g * GROUP + u // 2, (u % 2) * SUB:(u % 2 + 1) * SUB]
            s = jnp.dot(k, q, preferred_element_type=F32)
            dst[u * SUB:(u + 1) * SUB] = s
            m = jnp.max(s, axis=0, keepdims=True)
            most = m if most is None else jnp.maximum(most, m)
        return most

    def step(now, later, t, most):
        @pl.when(t < 7)
        def _():
            send_q(mirror(t + 1)).wait_recv()
            widen_q(q_in[t + 1], t + 1)

        @pl.when(t == 7)
        def _():
            for r in (4, 5, 7, 6):
                arrive(r)

        @pl.when(t == 15)
        def _():
            for r in range(4):
                arrive_next(r)

        @pl.when(t == 23)
        def _():
            for r in range(4, 8):
                arrive_next(r)

        i, g = where(t)
        old = top[i]
        new = jnp.maximum(old, most)
        top[i] = new
        i2, g2 = where(jnp.minimum(t + 1, 31))
        q = q_wide[i2]
        most = None
        mixed = None
        for u in range(TILE // SUB):
            rows = slice(u * SUB, (u + 1) * SUB)
            part = slice((u % 2) * SUB, (u % 2 + 1) * SUB)
            s = jnp.dot(k_wide[g2 * GROUP + u // 2, part], q, preferred_element_type=F32)
            later[rows] = s
            m = jnp.max(s, axis=0, keepdims=True)
            most = m if most is None else jnp.maximum(most, m)
            probs = jnp.exp2(now[rows] - new).astype(BF16)
            d = jnp.dot(v_in[g * GROUP + u // 2, :, part], probs, preferred_element_type=F32)
            mixed = d if mixed is None else mixed + d
        acc[i] = acc[i] * jnp.exp2(old - new) + mixed

        @pl.when(t >= 24)
        def _():
            a = acc[i]
            o = (a[0:HEAD_DIM] / a[HEAD_DIM:HEAD_DIM + 1]).astype(BF16)

            @pl.when(t < 31)
            def _():
                o_send[i] = o
                send_o(i).start()

            @pl.when(t == 31)
            def _():
                o_in[head] = o

        return most

    most = scores(s_even, 0)

    def two(n, most):
        most = step(s_even, s_odd, 2 * n, most)
        return step(s_odd, s_even, 2 * n + 1, most)

    lax.fori_loop(0, 16, two, most)

    for r in range(1, 8):
        p = peer(r)
        pltpu.make_async_remote_copy(
            src_ref=o_send.at[r], dst_ref=o_in.at[p], send_sem=o_ss.at[r], recv_sem=o_rs.at[p],
            device_id=(blk, p), device_id_type=MESH).wait_recv()
    mixed = o_in[...].reshape(WIDE, TOK)
    out_ref[...] = lax.dot_general(
        mixed, w_ref[...], (((0,), (0,)), ((), ())), preferred_element_type=F32
    ).astype(BF16)

    for r in range(1, 8):
        send_q(r).wait_send()
        send_k(r).wait_send()
        send_v(r).wait_send()
        send_o(r).wait_send()
    for r in range(8):
        pass_k(r).wait_send()
        pass_v(r).wait_send()


def on_device(queries, keys, values, w_out):
    vmem = pl.BlockSpec(memory_space=pltpu.VMEM)
    dma = pltpu.SemaphoreType.DMA
    return pl.pallas_call(
        kernel,
        out_shape=jax.ShapeDtypeStruct((TOK, WIDE), BF16),
        in_specs=[vmem] * 4,
        out_specs=vmem,
        scratch_shapes=[
            pltpu.VMEM((8, HEAD_DIM, TOK), BF16),
            pltpu.VMEM((8, TOK // 2, 128), BF16),
            pltpu.VMEM((8, HEAD_DIM, TOK), BF16),
            pltpu.VMEM((8, HEAD_DIM, TOK), BF16),
            pltpu.VMEM((16, TOK // 2, 128), BF16),
            pltpu.VMEM((16, VROWS, TOK), BF16),
            pltpu.VMEM((8, 2 * HEAD_DIM, TOK), BF16),
            pltpu.VMEM((16, TOK, 2 * HEAD_DIM), BF16),
            pltpu.VMEM((8, VROWS, TOK), F32),
            pltpu.VMEM((8, 1, TOK), F32),
            pltpu.VMEM((TILE, TOK), F32),
            pltpu.VMEM((TILE, TOK), F32),
            pltpu.VMEM((8, HEAD_DIM, TOK), BF16),
            pltpu.VMEM((8, HEAD_DIM, TOK), BF16),
            dma((8,)), dma((8,)), dma((16,)), dma((16,)),
            dma((16,)), dma((16,)), dma((8,)), dma((8,)),
        ],
        compiler_params=pltpu.CompilerParams(
            collective_id=0, has_side_effects=True, vmem_limit_bytes=48 * 2**20
        ),
        cost_estimate=pl.CostEstimate(
            flops=2 * 2 * TOK * WIDE * 16 * TOK + 2 * TOK * WIDE * WIDE,
            bytes_accessed=5 * TOK * WIDE * 2,
            transcendentals=TOK * HEADS * 16 * TOK,
        ),
    )(queries, keys, values, w_out)


def solution(mesh):
    split = P(("blk", "head"), None)
    return jax.shard_map(
        on_device, mesh=mesh, in_specs=(split, split, split, P()), out_specs=split, check_vma=False
    )
```

time: 483 us -> 73.2 us (0.15)
  waiting for transfers between devices: 226 us -> 0 us
  matrix products: 148 us -> 0 us
  other arithmetic: 84.3 us -> 0 us
  Pallas kernels: 0 us -> 67.9 us
  between operations: 13.4 us -> 0.01 us
    all_gather x2 -> x0, waiting for transfers between devices: 188 us -> none  [the longest x1 110 us: on_device(): lax.all_gather(keys, 'head', axis=0, tiled=True)]
    dot_general x17 -> x0, matrix products: 148 us -> none  [the longest x8 74.5 us: per_block(): jnp.dot(q_block, k_one.T, preferred_element_type=jnp.float32) * scaling]
    reduce_sum x8 -> x0, other arithmetic: 68.9 us -> none  [per_block(): total = jnp.sum(expo, axis=1, keepdims=True)]
    pallas_call x0 -> x1, Pallas kernels: none -> 67.9 us  [on_device(): pl.pallas_call(kernel, out_shape=jax.ShapeDtypeStruct((TOK, WIDE), BF16),...]
    ppermute x2 -> x0, waiting for transfers between devices: 37.4 us -> none  [from_behind(): lax.ppermute(array, axis, [(i, (i + by) % size) for i in range(size)])]
    concatenate x2 -> x0, other arithmetic: 15.4 us -> none  [the longest x1 7.69 us: on_device(): jnp.concatenate([group_v, next_v], axis=0).reshape(-1, HEADS, HEAD_DIM)]
  transfers between devices with their start and end apart: 4 -> 0, of which waited for: 3 -> 0; matrix products, arithmetic and copies ran while one was open for 2% -> 0% of each run, Pallas kernels for 0% -> 0%
where the time goes in v1:
time: 73.2 us; the launch traced here: 72.9 us
  Pallas kernels  67.9 us (93%)
  local copies, waits for them, and re-layouts  4.96 us (7%)
    pallas_call x1, Pallas kernels, on_device(): pl.pallas_call(kernel, out_shape=jax.ShapeDtypeStruct((TOK, WIDE), BF16),...  67.9 us
    unnamed x9, local copies, waits for them, and re-layouts  4.96 us

profile of v1, /device:TPU:224, one launch (start us, length us, event | category | flops | bytes accessed | tf_op | source)
XLA Modules:
  0.0 72.9 jit_solution(2956816544373037545)
XLA Ops:
  0.0 0.0 copy-start
  0.0 1.0 %copy-done = bf16[512,512]{1,0:T(8,128)(2,1)S(1)} copy-done((bf16[512,512]{1,0:T(8,128)(2,1)S(1)}, bf16[512,512]{1,0:T(8,128)(2,1)}, u32[]{:S(2)}) %copy-start) | copy-done | bytes 524312
  1.0 0.0 copy-start.1
  1.0 1.0 %copy-done.1 = bf16[512,512]{1,0:T(8,128)(2,1)S(1)} copy-done((bf16[512,512]{1,0:T(8,128)(2,1)S(1)}, bf16[512,512]{1,0:T(8,128)(2,1)}, u32[]{:S(2)}) %copy-start.1) | copy-done | bytes 524312
  2.1 0.0 copy-start.2
  2.1 1.0 %copy-done.2 = bf16[512,512]{1,0:T(8,128)(2,1)S(1)} copy-done((bf16[512,512]{1,0:T(8,128)(2,1)S(1)}, bf16[512,512]{1,0:T(8,128)(2,1)}, u32[]{:S(2)}) %copy-start.2) | copy-done | bytes 524312
  3.1 0.0 copy-start.3
  3.1 1.0 %copy-done.3 = bf16[512,512]{1,0:T(8,128)(2,1)S(1)} copy-done((bf16[512,512]{1,0:T(8,128)(2,1)S(1)}, bf16[512,512]{1,0:T(8,128)(2,1)}, u32[]{:S(2)}) %copy-start.3) | copy-done | bytes 524312
  4.2 67.9 %shard_map.46 = bf16[512,512]{1,0:T(8,128)(2,1)S(1)} custom-call(bf16[512,512]{1,0:T(8,128)(2,1)S(1)} %copy-done, bf16[512,512]{1,0:T(8,128)(2,1)S(1)} %copy-done.1, bf16[512,512]{1,0:T(8,128)(2,1)S(1)} %copy-done.2, bf16[512,512]{1,0:T(8,128)(2,1)S(1)} %copy-done.3), custom_call_target="tpu_custom_call" | custom-call | flops 8858370048 | bytes 2621440 | tf_op jit(solution)/shard_map/pallas_call | solution.py:261
  72.1 0.8 %copy.6 = bf16[512,512]{1,0:T(8,128)(2,1)} copy(bf16[512,512]{1,0:T(8,128)(2,1)S(1)} %shard_map.46) | data formatting | bytes 1048576
Async XLA Ops:
  0.0 1.0 %copy-start = (bf16[512,512]{1,0:T(8,128)(2,1)S(1)}, bf16[512,512]{1,0:T(8,128)(2,1)}, u32[]{:S(2)}) copy-start(bf16[512,512]{1,0:T(8,128)(2,1)} %q_ref.1) | copy-start | bytes 1572868
  1.0 1.0 %copy-start.1 = (bf16[512,512]{1,0:T(8,128)(2,1)S(1)}, bf16[512,512]{1,0:T(8,128)(2,1)}, u32[]{:S(2)}) copy-start(bf16[512,512]{1,0:T(8,128)(2,1)} %k_ref.1) | copy-start | bytes 1572868
  2.1 1.0 %copy-start.2 = (bf16[512,512]{1,0:T(8,128)(2,1)S(1)}, bf16[512,512]{1,0:T(8,128)(2,1)}, u32[]{:S(2)}) copy-start(bf16[512,512]{1,0:T(8,128)(2,1)} %v_ref.1) | copy-start | bytes 1572868
  3.1 1.0 %copy-start.3 = (bf16[512,512]{1,0:T(8,128)(2,1)S(1)}, bf16[512,512]{1,0:T(8,128)(2,1)}, u32[]{:S(2)}) copy-start(bf16[512,512]{1,0:T(8,128)(2,1)} %w_ref.1) | copy-start | bytes 1572868

commit v2 on v1

v2 whole, which is shorter than its diff:
```python
import jax
import jax.numpy as jnp
from jax import lax
from jax.experimental import pallas as pl
from jax.experimental.pallas import tpu as pltpu
from jax.sharding import PartitionSpec as P

HEADS = 8
HEAD_DIM = 64
TOK = 512
N_BLK = 32
WIDE = HEADS * HEAD_DIM
VROWS = 80
SUB = 256
GROUP = 4
TILE = GROUP * TOK
SCALE = 0.125 * 1.4426950408889634
F32 = jnp.float32
BF16 = jnp.bfloat16
MESH = pl.DeviceIdType.MESH
FAR = (0, 0, 0, 1, 0, 1, 1, 1)
NEAR = (0, 1, 3, 0, 2, 1, 3, 2)
MIRROR = (0, 2, 1, 3, 4, 6, 5, 7)
SECOND = range(4, 8)


def kernel(
    q_hbm, k_hbm, v_hbm, w_hbm, out_ref,
    q_ref, k_ref, v_ref, w_ref, load,
    kv_send, q_send, kv_in, q_in, q_wide, k_wide, v_wide,
    acc, top, s_even, s_odd, o_send, o_in,
    kv_ss, kv_rs, q_ss, q_rs, pass_ss, pass_rs, o_ss, o_rs,
):
    loads = [
        pltpu.make_async_copy(hbm, ref, load.at[n])
        for n, (hbm, ref) in enumerate(
            ((k_hbm, k_ref), (v_hbm, v_ref), (q_hbm, q_ref), (w_hbm, w_ref)))
    ]
    for copy in loads:
        copy.start()

    blk = lax.axis_index("blk")
    head = lax.axis_index("head")
    before = lax.rem(blk + N_BLK - 1, N_BLK)
    behind = lax.rem(blk + 1, N_BLK)

    def peer(r):
        far = lax.rem(head // 4 + FAR[r], 2)
        near = lax.rem(lax.rem(head, 4) + NEAR[r], 4)
        return far * 4 + near

    barrier = pltpu.get_barrier_semaphore()
    for r in range(1, 8):
        pl.semaphore_signal(barrier, inc=1, device_id=(blk, peer(r)), device_id_type=MESH)
    pl.semaphore_signal(barrier, inc=1, device_id=(behind, head), device_id_type=MESH)

    def remote(src, dst, send, recv, device):
        return pltpu.make_async_remote_copy(
            src_ref=src, dst_ref=dst, send_sem=send, recv_sem=recv,
            device_id=device, device_id_type=MESH)

    def send_q(r):
        p, s = peer(r), MIRROR[r]
        return remote(q_send.at[p], q_in.at[s], q_ss.at[r], q_rs.at[s], (blk, p))

    def send_kv(r):
        p, s = peer(r), MIRROR[r]
        return remote(kv_send.at[p], kv_in.at[s], kv_ss.at[r], kv_rs.at[s], (blk, p))

    def pass_kv(n):
        return remote(
            kv_in.at[pl.ds(4 * n, 4)], kv_in.at[pl.ds(8 + 4 * n, 4)],
            pass_ss.at[n], pass_rs.at[n], (before, head))

    def send_o(r):
        p = peer(r)
        return remote(o_send.at[r], o_in.at[head], o_ss.at[r], o_rs.at[head], (blk, p))

    left = lax.broadcasted_iota(jnp.int32, (HEAD_DIM, 128), 1) < HEAD_DIM
    half = TOK // 2

    def swap(x):
        return pltpu.roll(x, HEAD_DIM, 1)

    def transpose_into(src, dst, at):
        for pair in range(HEADS // 2):
            t = src[:, pair * 128:pair * 128 + 128].T
            dst[2 * pair, at:at + HEAD_DIM] = t[:HEAD_DIM]
            dst[2 * pair + 1, at:at + HEAD_DIM] = t[HEAD_DIM:]

    loads[0].wait()
    for pair in range(HEADS // 2):
        cols = slice(pair * 128, pair * 128 + 128)
        for c in range(4):
            a = k_ref[c * 64:c * 64 + 64, cols].astype(F32)
            b = k_ref[half + c * 64:half + c * 64 + 64, cols].astype(F32)
            lanes = slice(c * 128, c * 128 + 128)
            kv_send[2 * pair, 0:HEAD_DIM, lanes] = jnp.where(left, a, swap(b)).astype(BF16)
            kv_send[2 * pair + 1, 0:HEAD_DIM, lanes] = jnp.where(left, swap(a), b).astype(BF16)
    loads[1].wait()
    transpose_into(v_ref, kv_send, HEAD_DIM)
    pl.semaphore_wait(barrier, 8)
    for r in (1, 2, 3):
        send_kv(r).start()
    loads[2].wait()
    transpose_into(q_ref, q_send, 0)
    for r in range(1, 8):
        send_q(r).start()

    def widen_q(q, s):
        scaled = q.astype(F32) * SCALE
        high = scaled.astype(BF16)
        q_wide[s, 0:HEAD_DIM] = high
        q_wide[s, HEAD_DIM:2 * HEAD_DIM] = (scaled - high.astype(F32)).astype(BF16)

    def widen_kv(s):
        for c in range(4):
            x = kv_in[s, 0:HEAD_DIM, c * 128:c * 128 + 128].astype(F32)
            y = swap(x)
            k_wide[s, c * 64:c * 64 + 64] = jnp.where(left, x, y).astype(BF16)
            k_wide[s, half + c * 64:half + c * 64 + 64] = jnp.where(left, y, x).astype(BF16)
        v_wide[s, 0:HEAD_DIM] = kv_in[s, HEAD_DIM:2 * HEAD_DIM]

    kv_in[0] = kv_send[head]
    for s in range(16):
        v_wide[s, HEAD_DIM:VROWS] = jnp.ones((VROWS - HEAD_DIM, TOK), BF16)
    acc[...] = jnp.zeros_like(acc)
    top[...] = jnp.full(top.shape, -1e30, F32)
    widen_q(q_send[head], 0)
    widen_kv(0)

    def arrive(n):
        for r in range(4 * n, 4 * n + 4):
            if r > 0:
                send_kv(MIRROR[r]).wait_recv()
                widen_kv(r)

    def arrive_next(n):
        pass_kv(n).wait_recv()
        for r in range(8 + 4 * n, 12 + 4 * n):
            widen_kv(r)

    arrive(0)
    for r in SECOND:
        send_kv(r).start()

    def where(t):
        second = t // 16
        u = t % 16
        c = u // 7
        up = (1 - c) * (2 - c) // 2
        down = c * (2 - c)
        own = c * (c - 1) // 2
        i = (1 - second) * (u % 8) + second * (up * (u + 1) + down * (14 - u))
        g = (1 - second) * (u // 8) + second * (2 * up + 3 * down + own * (u - 12))
        return i, g

    def tile(dst, t, src, t_src, new):
        i, g = where(t)
        q = q_wide[i]
        if src is not None:
            g_src = where(t_src)[1]
        most = mixed = None
        for u in range(TILE // SUB):
            rows = slice(u * SUB, (u + 1) * SUB)
            part = slice((u % 2) * SUB, (u % 2 + 1) * SUB)
            s = jnp.dot(k_wide[g * GROUP + u // 2, part], q, preferred_element_type=F32)
            dst[rows] = s
            m = jnp.max(s, axis=0, keepdims=True)
            most = m if most is None else jnp.maximum(most, m)
            if src is not None:
                probs = jnp.exp2(src[rows] - new).astype(BF16)
                d = jnp.dot(
                    v_wide[g_src * GROUP + u // 2, :, part], probs, preferred_element_type=F32)
                mixed = d if mixed is None else mixed + d
        return most, mixed

    def step(now, later, t, most):
        @pl.when(t < 7)
        def _():
            r = t + 1
            remote(q_send.at[r], q_in.at[r], q_ss.at[r], q_rs.at[r], (before, head)).wait_recv()
            widen_q(q_in[r], r)

        @pl.when(t == 7)
        def _():
            arrive(1)
            pass_kv(0).start()

        @pl.when(t == 11)
        def _():
            pass_kv(1).start()

        @pl.when(t == 15)
        def _():
            arrive_next(0)

        @pl.when(t == 22)
        def _():
            arrive_next(1)

        i = where(t)[0]
        old = top[i]
        new = jnp.maximum(old, most)
        top[i] = new
        most, mixed = tile(later, (t + 1) % 32, now, t, new)
        acc[i] = acc[i] * jnp.exp2(old - new) + mixed

        @pl.when(t >= 23)
        def _():
            a = acc[i]
            o_send[i] = (a[0:HEAD_DIM] / a[HEAD_DIM:HEAD_DIM + 1]).astype(BF16)

        for r in range(1, 8):
            @pl.when(t == 30 - r)
            def _():
                send_o(r).start()

        return most

    most, _ = tile(s_even, 0, None, 0, None)

    def two(n, most):
        most = step(s_even, s_odd, 2 * n, most)
        return step(s_odd, s_even, 2 * n + 1, most)

    lax.fori_loop(0, 16, two, most)

    o_in[head] = o_send[0]
    loads[3].wait()
    for r in range(1, 8):
        p = peer(r)
        remote(o_send.at[r], o_in.at[p], o_ss.at[r], o_rs.at[p], (blk, p)).wait_recv()
    mixed = o_in[...].reshape(WIDE, TOK)
    out_ref[...] = lax.dot_general(
        mixed, w_ref[...], (((0,), (0,)), ((), ())), preferred_element_type=F32
    ).astype(BF16)

    for r in range(1, 8):
        send_q(r).wait_send()
        send_kv(r).wait_send()
        send_o(r).wait_send()
    for n in range(2):
        pass_kv(n).wait_send()


def on_device(queries, keys, values, w_out):
    vmem = pl.BlockSpec(memory_space=pltpu.VMEM)
    hbm = pl.BlockSpec(memory_space=pltpu.HBM)
    dma = pltpu.SemaphoreType.DMA
    return pl.pallas_call(
        kernel,
        out_shape=jax.ShapeDtypeStruct((TOK, WIDE), BF16),
        in_specs=[hbm] * 4,
        out_specs=vmem,
        scratch_shapes=[
            *[pltpu.VMEM((TOK, WIDE), BF16)] * 4,
            dma((4,)),
            pltpu.VMEM((8, 2 * HEAD_DIM, TOK), BF16),
            pltpu.VMEM((8, HEAD_DIM, TOK), BF16),
            pltpu.VMEM((16, 2 * HEAD_DIM, TOK), BF16),
            pltpu.VMEM((8, HEAD_DIM, TOK), BF16),
            pltpu.VMEM((8, 2 * HEAD_DIM, TOK), BF16),
            pltpu.VMEM((16, TOK, 2 * HEAD_DIM), BF16),
            pltpu.VMEM((16, VROWS, TOK), BF16),
            pltpu.VMEM((8, VROWS, TOK), F32),
            pltpu.VMEM((8, 1, TOK), F32),
            pltpu.VMEM((TILE, TOK), F32),
            pltpu.VMEM((TILE, TOK), F32),
            pltpu.VMEM((8, HEAD_DIM, TOK), BF16),
            pltpu.VMEM((8, HEAD_DIM, TOK), BF16),
            dma((8,)), dma((8,)), dma((8,)), dma((8,)),
            dma((2,)), dma((2,)), dma((8,)), dma((8,)),
        ],
        compiler_params=pltpu.CompilerParams(
            collective_id=0, has_side_effects=True, vmem_limit_bytes=48 * 2**20
        ),
        cost_estimate=pl.CostEstimate(
            flops=2 * 2 * TOK * WIDE * 16 * TOK + 2 * TOK * WIDE * WIDE,
            bytes_accessed=5 * TOK * WIDE * 2,
            transcendentals=TOK * HEADS * 16 * TOK,
        ),
    )(queries, keys, values, w_out)


def solution(mesh):
    split = P(("blk", "head"), None)
    return jax.shard_map(
        on_device, mesh=mesh, in_specs=(split, split, split, P()), out_specs=split, check_vma=False
    )
```

time: 73.2 us -> 61.1 us (0.83)
  Pallas kernels: 67.9 us -> 55.2 us
    pallas_call x1, Pallas kernels: 67.9 us -> 55.2 us  [on_device(): pl.pallas_call(kernel, out_shape=jax.ShapeDtypeStruct((TOK, WIDE), BF16),...]
where the time goes in v2:
time: 61.1 us; the launch traced here: 60.1 us
  Pallas kernels  55.2 us (90%)
  local copies, waits for them, and re-layouts  4.96 us (8%)
    pallas_call x1, Pallas kernels, on_device(): pl.pallas_call(kernel, out_shape=jax.ShapeDtypeStruct((TOK, WIDE), BF16),...  55.2 us
    unnamed x9, local copies, waits for them, and re-layouts  4.96 us

profile of v2, /device:TPU:224, one launch (start us, length us, event | category | flops | bytes accessed | tf_op | source)
XLA Modules:
  0.0 60.1 jit_solution(3507384567155635559)
XLA Ops:
  0.0 0.0 copy-start
  0.0 1.0 %copy-done = bf16[512,512]{1,0:T(8,128)(2,1)S(1)} copy-done((bf16[512,512]{1,0:T(8,128)(2,1)S(1)}, bf16[512,512]{1,0:T(8,128)(2,1)}, u32[]{:S(2)}) %copy-start) | copy-done | bytes 524312
  1.0 0.0 copy-start.1
  1.0 1.0 %copy-done.1 = bf16[512,512]{1,0:T(8,128)(2,1)S(1)} copy-done((bf16[512,512]{1,0:T(8,128)(2,1)S(1)}, bf16[512,512]{1,0:T(8,128)(2,1)}, u32[]{:S(2)}) %copy-start.1) | copy-done | bytes 524312
  2.1 0.0 copy-start.2
  2.1 1.0 %copy-done.2 = bf16[512,512]{1,0:T(8,128)(2,1)S(1)} copy-done((bf16[512,512]{1,0:T(8,128)(2,1)S(1)}, bf16[512,512]{1,0:T(8,128)(2,1)}, u32[]{:S(2)}) %copy-start.2) | copy-done | bytes 524312
  3.1 0.0 copy-start.3
  3.1 1.0 %copy-done.3 = bf16[512,512]{1,0:T(8,128)(2,1)S(1)} copy-done((bf16[512,512]{1,0:T(8,128)(2,1)S(1)}, bf16[512,512]{1,0:T(8,128)(2,1)}, u32[]{:S(2)}) %copy-start.3) | copy-done | bytes 524312
  4.2 55.2 %shard_map.46 = bf16[512,512]{1,0:T(8,128)(2,1)S(1)} custom-call(bf16[512,512]{1,0:T(8,128)(2,1)S(1)} %copy-done, bf16[512,512]{1,0:T(8,128)(2,1)S(1)} %copy-done.1, bf16[512,512]{1,0:T(8,128)(2,1)S(1)} %copy-done.2, bf16[512,512]{1,0:T(8,128)(2,1)S(1)} %copy-done.3), custom_call_target="tpu_custom_call" | custom-call | flops 8858370048 | bytes 2621440 | tf_op jit(solution)/shard_map/pallas_call | solution.py:251
  59.3 0.8 %copy.6 = bf16[512,512]{1,0:T(8,128)(2,1)} copy(bf16[512,512]{1,0:T(8,128)(2,1)S(1)} %shard_map.46) | data formatting | bytes 1048576
Async XLA Ops:
  0.0 1.0 %copy-start = (bf16[512,512]{1,0:T(8,128)(2,1)S(1)}, bf16[512,512]{1,0:T(8,128)(2,1)}, u32[]{:S(2)}) copy-start(bf16[512,512]{1,0:T(8,128)(2,1)} %q_hbm.1) | copy-start | bytes 1572868
  1.0 1.0 %copy-start.1 = (bf16[512,512]{1,0:T(8,128)(2,1)S(1)}, bf16[512,512]{1,0:T(8,128)(2,1)}, u32[]{:S(2)}) copy-start(bf16[512,512]{1,0:T(8,128)(2,1)} %k_hbm.1) | copy-start | bytes 1572868
  2.1 1.0 %copy-start.2 = (bf16[512,512]{1,0:T(8,128)(2,1)S(1)}, bf16[512,512]{1,0:T(8,128)(2,1)}, u32[]{:S(2)}) copy-start(bf16[512,512]{1,0:T(8,128)(2,1)} %v_hbm.1) | copy-start | bytes 1572868
  3.1 1.0 %copy-start.3 = (bf16[512,512]{1,0:T(8,128)(2,1)S(1)}, bf16[512,512]{1,0:T(8,128)(2,1)}, u32[]{:S(2)}) copy-start(bf16[512,512]{1,0:T(8,128)(2,1)} %w_hbm.1) | copy-start | bytes 1572868

commit v3 on v2

--- a/solution.py
+++ b/solution.py
@@ -36,23 +36,25 @@
         for n, (hbm, ref) in enumerate(
             ((k_hbm, k_ref), (v_hbm, v_ref), (q_hbm, q_ref), (w_hbm, w_ref)))
     ]
-    for copy in loads:
-        copy.start()
-
     blk = lax.axis_index("blk")
     head = lax.axis_index("head")
     before = lax.rem(blk + N_BLK - 1, N_BLK)
     behind = lax.rem(blk + 1, N_BLK)
 
+    x, y = lax.div(head, 4), lax.rem(head, 4)
+    peers = [lax.rem(x + f, 2) * 4 + lax.rem(y + n, 4) for f, n in zip(FAR, NEAR)]
+
     def peer(r):
-        far = lax.rem(head // 4 + FAR[r], 2)
-        near = lax.rem(lax.rem(head, 4) + NEAR[r], 4)
-        return far * 4 + near
-
+        return peers[r]
+
+    for copy in loads[:2]:
+        copy.start()
     barrier = pltpu.get_barrier_semaphore()
     for r in range(1, 8):
         pl.semaphore_signal(barrier, inc=1, device_id=(blk, peer(r)), device_id_type=MESH)
     pl.semaphore_signal(barrier, inc=1, device_id=(behind, head), device_id_type=MESH)
+    for copy in loads[2:]:
+        copy.start()
 
     def remote(src, dst, send, recv, device):
         return pltpu.make_async_remote_copy(
@@ -141,19 +143,14 @@
             widen_kv(r)
 
     arrive(0)
-    for r in SECOND:
-        send_kv(r).start()
+
+    pass_kv(0).start()
 
     def where(t):
-        second = t // 16
-        u = t % 16
-        c = u // 7
-        up = (1 - c) * (2 - c) // 2
-        down = c * (2 - c)
-        own = c * (c - 1) // 2
-        i = (1 - second) * (u % 8) + second * (up * (u + 1) + down * (14 - u))
-        g = (1 - second) * (u // 8) + second * (2 * up + 3 * down + own * (u - 12))
-        return i, g
+        n = (t >= 8).astype(jnp.int32) + (t >= 15).astype(jnp.int32) + (t >= 22).astype(jnp.int32)
+        i = jnp.where(t >= 29, 0, jnp.where(t >= 22, 29 - t, t - 7 * n))
+        g = jnp.where(t >= 29, t - 28, n)
+        return i, jnp.where(g == 1, 2, jnp.where(g == 2, 1, g))
 
     def tile(dst, t, src, t_src, new):
         i, g = where(t)
@@ -182,43 +179,44 @@
             remote(q_send.at[r], q_in.at[r], q_ss.at[r], q_rs.at[r], (before, head)).wait_recv()
             widen_q(q_in[r], r)
 
-        @pl.when(t == 7)
-        def _():
+        def at(when, act):
+            @pl.when(t == when)
+            def _():
+                act()
+
+        def rest():
+            for r in SECOND:
+                send_kv(r).start()
+
+        def far_arrive():
             arrive(1)
-            pass_kv(0).start()
-
-        @pl.when(t == 11)
-        def _():
             pass_kv(1).start()
 
-        @pl.when(t == 15)
-        def _():
-            arrive_next(0)
-
-        @pl.when(t == 22)
-        def _():
-            arrive_next(1)
+        at(3, rest)
+        at(7, lambda: arrive_next(0))
+        at(12, far_arrive)
+        at(21, lambda: arrive_next(1))
 
         i = where(t)[0]
         old = top[i]
         new = jnp.maximum(old, most)
         top[i] = new
-        most, mixed = tile(later, (t + 1) % 32, now, t, new)
+        most, mixed = tile(later, jnp.minimum(t + 1, 31), now, t, new)
         acc[i] = acc[i] * jnp.exp2(old - new) + mixed
 
-        @pl.when(t >= 23)
+        @pl.when(t >= 22)
         def _():
             a = acc[i]
             o_send[i] = (a[0:HEAD_DIM] / a[HEAD_DIM:HEAD_DIM + 1]).astype(BF16)
 
         for r in range(1, 8):
-            @pl.when(t == 30 - r)
+            @pl.when(t == 29 - r)
             def _():
                 send_o(r).start()
 
         return most
 
-    most, _ = tile(s_even, 0, None, 0, None)
+    most, _ = tile(s_even, jnp.int32(0), None, 0, None)
 
     def two(n, most):
         most = step(s_even, s_odd, 2 * n, most)

time: 61.1 us -> 59.8 us (0.979)
  Pallas kernels: 55.2 us -> 53.9 us
    pallas_call x1, Pallas kernels: 55.2 us -> 53.9 us  [on_device(): pl.pallas_call(kernel, out_shape=jax.ShapeDtypeStruct((TOK, WIDE), BF16),...]
where the time goes in v3:
time: 59.8 us; the launch traced here: 58.9 us
  Pallas kernels  53.9 us (90%)
  local copies, waits for them, and re-layouts  4.96 us (8%)
    pallas_call x1, Pallas kernels, on_device(): pl.pallas_call(kernel, out_shape=jax.ShapeDtypeStruct((TOK, WIDE), BF16),...  53.9 us
    unnamed x9, local copies, waits for them, and re-layouts  4.96 us

profile of v3, /device:TPU:224, one launch (start us, length us, event | category | flops | bytes accessed | tf_op | source)
XLA Modules:
  0.0 58.9 jit_solution(17243205008594556357)
XLA Ops:
  0.0 0.0 copy-start
  0.0 1.0 %copy-done = bf16[512,512]{1,0:T(8,128)(2,1)S(1)} copy-done((bf16[512,512]{1,0:T(8,128)(2,1)S(1)}, bf16[512,512]{1,0:T(8,128)(2,1)}, u32[]{:S(2)}) %copy-start) | copy-done | bytes 524312
  1.0 0.0 copy-start.1
  1.0 1.0 %copy-done.1 = bf16[512,512]{1,0:T(8,128)(2,1)S(1)} copy-done((bf16[512,512]{1,0:T(8,128)(2,1)S(1)}, bf16[512,512]{1,0:T(8,128)(2,1)}, u32[]{:S(2)}) %copy-start.1) | copy-done | bytes 524312
  2.1 0.0 copy-start.2
  2.1 1.0 %copy-done.2 = bf16[512,512]{1,0:T(8,128)(2,1)S(1)} copy-done((bf16[512,512]{1,0:T(8,128)(2,1)S(1)}, bf16[512,512]{1,0:T(8,128)(2,1)}, u32[]{:S(2)}) %copy-start.2) | copy-done | bytes 524312
  3.1 0.0 copy-start.3
  3.1 1.0 %copy-done.3 = bf16[512,512]{1,0:T(8,128)(2,1)S(1)} copy-done((bf16[512,512]{1,0:T(8,128)(2,1)S(1)}, bf16[512,512]{1,0:T(8,128)(2,1)}, u32[]{:S(2)}) %copy-start.3) | copy-done | bytes 524312
  4.2 53.9 %shard_map.46 = bf16[512,512]{1,0:T(8,128)(2,1)S(1)} custom-call(bf16[512,512]{1,0:T(8,128)(2,1)S(1)} %copy-done, bf16[512,512]{1,0:T(8,128)(2,1)S(1)} %copy-done.1, bf16[512,512]{1,0:T(8,128)(2,1)S(1)} %copy-done.2, bf16[512,512]{1,0:T(8,128)(2,1)S(1)} %copy-done.3), custom_call_target="tpu_custom_call" | custom-call | flops 8858370048 | bytes 2621440 | tf_op jit(solution)/shard_map/pallas_call | solution.py:249
  58.1 0.8 %copy.6 = bf16[512,512]{1,0:T(8,128)(2,1)} copy(bf16[512,512]{1,0:T(8,128)(2,1)S(1)} %shard_map.46) | data formatting | bytes 1048576
Async XLA Ops:
  0.0 1.0 %copy-start = (bf16[512,512]{1,0:T(8,128)(2,1)S(1)}, bf16[512,512]{1,0:T(8,128)(2,1)}, u32[]{:S(2)}) copy-start(bf16[512,512]{1,0:T(8,128)(2,1)} %q_hbm.1) | copy-start | bytes 1572868
  1.0 1.0 %copy-start.1 = (bf16[512,512]{1,0:T(8,128)(2,1)S(1)}, bf16[512,512]{1,0:T(8,128)(2,1)}, u32[]{:S(2)}) copy-start(bf16[512,512]{1,0:T(8,128)(2,1)} %k_hbm.1) | copy-start | bytes 1572868
  2.1 1.0 %copy-start.2 = (bf16[512,512]{1,0:T(8,128)(2,1)S(1)}, bf16[512,512]{1,0:T(8,128)(2,1)}, u32[]{:S(2)}) copy-start(bf16[512,512]{1,0:T(8,128)(2,1)} %v_hbm.1) | copy-start | bytes 1572868
  3.1 1.0 %copy-start.3 = (bf16[512,512]{1,0:T(8,128)(2,1)S(1)}, bf16[512,512]{1,0:T(8,128)(2,1)}, u32[]{:S(2)}) copy-start(bf16[512,512]{1,0:T(8,128)(2,1)} %w_hbm.1) | copy-start | bytes 1572868

commit v4 on v3

--- a/solution.py
+++ b/solution.py
@@ -132,10 +132,12 @@
     widen_kv(0)
 
     def arrive(n):
-        for r in range(4 * n, 4 * n + 4):
-            if r > 0:
-                send_kv(MIRROR[r]).wait_recv()
-                widen_kv(r)
+        fresh = [r for r in range(4 * n, 4 * n + 4) if r > 0]
+        for r in fresh:
+            send_kv(MIRROR[r]).wait_recv()
+        pass_kv(n).start()
+        for r in fresh:
+            widen_kv(r)
 
     def arrive_next(n):
         pass_kv(n).wait_recv()
@@ -143,8 +145,6 @@
             widen_kv(r)
 
     arrive(0)
-
-    pass_kv(0).start()
 
     def where(t):
         n = (t >= 8).astype(jnp.int32) + (t >= 15).astype(jnp.int32) + (t >= 22).astype(jnp.int32)
@@ -190,7 +190,6 @@
 
         def far_arrive():
             arrive(1)
-            pass_kv(1).start()
 
         at(3, rest)
         at(7, lambda: arrive_next(0))

time: 59.8 us -> 60.1 us (level)
  no operation moved by 1% of the time
where the time goes in v4:
time: 60.1 us; the launch traced here: 59.1 us
  Pallas kernels  54.1 us (90%)
  local copies, waits for them, and re-layouts  4.96 us (8%)
    pallas_call x1, Pallas kernels, on_device(): pl.pallas_call(kernel, out_shape=jax.ShapeDtypeStruct((TOK, WIDE), BF16),...  54.1 us
    unnamed x9, local copies, waits for them, and re-layouts  4.96 us

profile of v4, /device:TPU:224, one launch (start us, length us, event | category | flops | bytes accessed | tf_op | source)
XLA Modules:
  0.0 59.1 jit_solution(15109560076809814256)
XLA Ops:
  0.0 0.0 copy-start
  0.0 1.0 %copy-done = bf16[512,512]{1,0:T(8,128)(2,1)S(1)} copy-done((bf16[512,512]{1,0:T(8,128)(2,1)S(1)}, bf16[512,512]{1,0:T(8,128)(2,1)}, u32[]{:S(2)}) %copy-start) | copy-done | bytes 524312
  1.0 0.0 copy-start.1
  1.0 1.0 %copy-done.1 = bf16[512,512]{1,0:T(8,128)(2,1)S(1)} copy-done((bf16[512,512]{1,0:T(8,128)(2,1)S(1)}, bf16[512,512]{1,0:T(8,128)(2,1)}, u32[]{:S(2)}) %copy-start.1) | copy-done | bytes 524312
  2.1 0.0 copy-start.2
  2.1 1.0 %copy-done.2 = bf16[512,512]{1,0:T(8,128)(2,1)S(1)} copy-done((bf16[512,512]{1,0:T(8,128)(2,1)S(1)}, bf16[512,512]{1,0:T(8,128)(2,1)}, u32[]{:S(2)}) %copy-start.2) | copy-done | bytes 524312
  3.1 0.0 copy-start.3
  3.1 1.0 %copy-done.3 = bf16[512,512]{1,0:T(8,128)(2,1)S(1)} copy-done((bf16[512,512]{1,0:T(8,128)(2,1)S(1)}, bf16[512,512]{1,0:T(8,128)(2,1)}, u32[]{:S(2)}) %copy-start.3) | copy-done | bytes 524312
  4.2 54.1 %shard_map.46 = bf16[512,512]{1,0:T(8,128)(2,1)S(1)} custom-call(bf16[512,512]{1,0:T(8,128)(2,1)S(1)} %copy-done, bf16[512,512]{1,0:T(8,128)(2,1)S(1)} %copy-done.1, bf16[512,512]{1,0:T(8,128)(2,1)S(1)} %copy-done.2, bf16[512,512]{1,0:T(8,128)(2,1)S(1)} %copy-done.3), custom_call_target="tpu_custom_call" | custom-call | flops 8858370048 | bytes 2621440 | tf_op jit(solution)/shard_map/pallas_call | solution.py:248
  58.3 0.8 %copy.6 = bf16[512,512]{1,0:T(8,128)(2,1)} copy(bf16[512,512]{1,0:T(8,128)(2,1)S(1)} %shard_map.46) | data formatting | bytes 1048576
Async XLA Ops:
  0.0 1.0 %copy-start = (bf16[512,512]{1,0:T(8,128)(2,1)S(1)}, bf16[512,512]{1,0:T(8,128)(2,1)}, u32[]{:S(2)}) copy-start(bf16[512,512]{1,0:T(8,128)(2,1)} %q_hbm.1) | copy-start | bytes 1572868
  1.0 1.0 %copy-start.1 = (bf16[512,512]{1,0:T(8,128)(2,1)S(1)}, bf16[512,512]{1,0:T(8,128)(2,1)}, u32[]{:S(2)}) copy-start(bf16[512,512]{1,0:T(8,128)(2,1)} %k_hbm.1) | copy-start | bytes 1572868
  2.1 1.0 %copy-start.2 = (bf16[512,512]{1,0:T(8,128)(2,1)S(1)}, bf16[512,512]{1,0:T(8,128)(2,1)}, u32[]{:S(2)}) copy-start(bf16[512,512]{1,0:T(8,128)(2,1)} %v_hbm.1) | copy-start | bytes 1572868
  3.1 1.0 %copy-start.3 = (bf16[512,512]{1,0:T(8,128)(2,1)S(1)}, bf16[512,512]{1,0:T(8,128)(2,1)}, u32[]{:S(2)}) copy-start(bf16[512,512]{1,0:T(8,128)(2,1)} %w_hbm.1) | copy-start | bytes 1572868
